TPU v7x, 32 devices: a whole 2x2x4 slice. The times are simulated.
32 devices in a mesh: groups: 2 (over x), tm: 16 (over z, y, core).
Axes of the slice: x: 2, y: 2, z: 4, core: 2. Of those that a mesh axis runs over, the one named last changes fastest.
Arguments:
- hidden: bfloat16 [1024, 512], P(('groups', 'tm')), parts along dimension 0, may hold values from -6 to 6
- durations: int32 [1024], P(('groups', 'tm')), parts along dimension 0, may hold values from 1 to 99, as said below
- mel_weight: bfloat16 [512, 80], replicated, may hold values from -0.25 to 0.25
- mel_bias: float32 [80], replicated, may hold values from -3 to 3
- pre_weight: bfloat16 [7, 80, 512], replicated, may hold values from -0.25 to 0.25
- pre_bias: float32 [512], replicated, may hold values from -3 to 3
- up_weight: bfloat16 [512, 16, 256], replicated, may hold values from -0.1875 to 0.1875
- up_bias: float32 [256], replicated, may hold values from -3 to 3
- res_weight: bfloat16 [4, 3, 256, 256], replicated, may hold values from -0.21875 to 0.21875
- res_bias: float32 [4, 256], replicated, may hold values from -3 to 3
Outputs:
- features: bfloat16 [262144, 256], P(('groups', 'tm')), parts along dimension 0
There are 2 independent parts, one for each index of `groups`. A program takes and returns all parts, laid end to end along the dimension named above; an argument that names none is the same for every part. Nothing has to cross between parts.
Inputs may be any that keep to these rules, and one draw needn't show every extreme that they name: Every duration is 1 or more; the durations of the chapter sum to 16384; the phonemes of device j (rows j * 32 to (j + 1) * 32 - 1) span between 512 and 1536 frames, and the first frame of device j's phonemes lies within 256 of j * 1024, reached on some device in every draw, so that the frames of device j are covered only by phonemes of devices j - 1, j and j + 1.
All inputs are finite; a program needn't handle non-finite values.
Results may differ from a plain program's by a relative error of at most 0.01.
Values may be sent and summed in bfloat16 or wider, within the bound.
A program may use at most 128 MiB of HBM per device.

v0:
```python
import jax
import jax.numpy as jnp
from jax import lax
from jax.sharding import PartitionSpec as P

FR_DEV = 1024


def with_halo(block, sides, width):
    for axis, dim in sides:
        count = lax.axis_size(axis)
        forward = [(i, i + 1) for i in range(count - 1)]
        backward = [(target, source) for source, target in forward]
        low = lax.ppermute(
            lax.slice_in_dim(block, block.shape[dim] - width, None, axis=dim), axis, forward
        )
        high = lax.ppermute(lax.slice_in_dim(block, 0, width, axis=dim), axis, backward)
        block = jnp.concatenate([low, block, high], axis=dim)
    return block


def entering(part, axis, combine, identity):
    place = lax.axis_index(axis)
    gathered = lax.all_gather(part, axis)
    state = jnp.zeros_like(part) + jnp.asarray(identity, part.dtype)

    def one(hop, state):
        return combine(state, lax.dynamic_index_in_dim(gathered, hop, 0, False))

    return lax.fori_loop(0, place, one, state)


def leaky(v):
    return jnp.where(v >= 0, v, 0.1 * v)


def add_counts(earlier, later):
    return earlier + later


def tap_sum(padded, weight, dilation, length):
    total = jnp.dot(padded[0:length], weight[0], preferred_element_type=jnp.float32)
    for k in range(1, weight.shape[0]):
        total = total + jnp.dot(
            padded[k * dilation : k * dilation + length],
            weight[k],
            preferred_element_type=jnp.float32,
        )
    return total


def expand_rows(frame_ids, rows, bounds):
    inside = (frame_ids[:, None] >= bounds[None, :, 0]) & (frame_ids[:, None] < bounds[None, :, 1])
    return jnp.dot(inside.astype(jnp.bfloat16), rows, preferred_element_type=jnp.float32)


def residual_conv(state, weight, bias, dilation):
    padded = with_halo(state, (("tm", 0),), dilation)
    return tap_sum(padded, weight, dilation, state.shape[0]) + bias


def upsample(act_rows, up_weight, up_bias, count):
    channels_in, taps_count, channels_out = up_weight.shape
    taps = jnp.dot(
        act_rows,
        up_weight.reshape(channels_in, taps_count * channels_out),
        preferred_element_type=jnp.float32,
    )
    taps = taps.reshape(count + 2, taps_count, channels_out)
    lower = taps[1 : count + 1, 4:8] + taps[0:count, 12:16]
    upper = taps[1 : count + 1, 8:12] + taps[2 : count + 2, 0:4]
    joined = jnp.concatenate([lower, upper], axis=1) + up_bias
    return joined.reshape(count * 8, channels_out).astype(jnp.bfloat16)


def on_device(
    hidden,
    durations,
    mel_weight,
    mel_bias,
    pre_weight,
    pre_bias,
    up_weight,
    up_bias,
    res_weight,
    res_bias,
):
    phonemes, width = hidden.shape
    frames = FR_DEV
    device = lax.axis_index("tm")
    block_total = jnp.sum(durations)
    offset = entering(block_total, "tm", add_counts, jnp.int32(0))
    ends = offset + jnp.cumsum(durations)
    bounds = jnp.stack([ends - durations, ends], axis=1).astype(jnp.int32)
    extra = 0
    rows_count = frames + 2 * extra
    frame_ids = device * frames - extra + jnp.arange(rows_count, dtype=jnp.int32)
    rows_near, bounds_near = (
        with_halo(hidden, (("tm", 0),), phonemes),
        with_halo(bounds, (("tm", 0),), phonemes),
    )
    spread = expand_rows(frame_ids, rows_near, bounds_near)
    expanded = spread.astype(jnp.bfloat16)
    mel_full = jnp.dot(expanded, mel_weight, preferred_element_type=jnp.float32) + mel_bias
    mel = mel_full.astype(jnp.bfloat16)
    mel_wide = with_halo(mel, (("tm", 0),), 3)
    pre = tap_sum(mel_wide, pre_weight, 1, frames) + pre_bias
    act = leaky(pre).astype(jnp.bfloat16)
    act_wide = with_halo(act, (("tm", 0),), 1)
    upsampled = upsample(act_wide, up_weight, up_bias, frames)
    state = upsampled
    for pair, dilation in enumerate((1, 3)):
        inner = leaky(state.astype(jnp.float32)).astype(jnp.bfloat16)
        first = leaky(
            residual_conv(inner, res_weight[2 * pair], res_bias[2 * pair], dilation)
        ).astype(jnp.bfloat16)
        second = residual_conv(first, res_weight[2 * pair + 1], res_bias[2 * pair + 1], 1)
        state = (state.astype(jnp.float32) + second).astype(jnp.bfloat16)
    return state


def solution(mesh):
    in_specs = (
        P(("groups", "tm"), None),
        P(("groups", "tm")),
        P(),
        P(),
        P(),
        P(),
        P(),
        P(),
        P(),
        P(),
    )
    out_specs = P(("groups", "tm"), None)
    return jax.shard_map(
        on_device, mesh=mesh, in_specs=in_specs, out_specs=out_specs, check_vma=False
    )
```

profile of v0, /device:TPU:21, one launch (start us, length us, event | category | flops | bytes accessed | tf_op | source)
XLA Modules:
  0.0 202.3 jit_solution(383772836343033844)
XLA Ops:
  0.0 1.4 reduce_sum.9
  1.4 1.3 dynamic-slice
  2.7 1.5 dynamic-update-slice
  4.2 6.6 %all-reduce = s32[16]{0:T(128)S(1)} all-reduce(s32[16]{0:T(128)S(1)} %dynamic-update-slice), channel_id=1, replica_groups=mesh['groups'=2,'tm'=16] {'tm'}, use_global_device_ids=true, to_apply=%add | all-reduce | flops 16 | bytes 128
  10.8 14.8 %while.10 = (s32[]{:T(128)}, s32[]{:T(128)}, s32[]{:T(128)}, s32[16]{0:T(128)S(1)}, s32[]{:T(128)}, /*index=5*/s32[]{:T(128)}, s32[]{:T(128)}) while((s32[]{:T(128)}, s32[]{:T(128)}, s32[]{:T(128)}, s32[16]{0:T(128)S(1)}, s32[]{:T(128)}, /*index=5*/s32[]{:T(128)}, s32[]{:T(128)}) %tuple.32), condition=%wide.region_2.3_spmd, body=%wide.region_1.2_spmd.sunk | while | flops 6 | bytes 143 | solution.py:30
  10.8 0.6 dynamic_slice.5
  12.2 0.7 dynamic_slice.5
  13.5 0.7 dynamic_slice.5
  14.9 0.7 dynamic_slice.5
  16.2 0.7 dynamic_slice.5
  17.6 0.7 dynamic_slice.5
  18.9 0.7 dynamic_slice.5
  20.3 0.7 dynamic_slice.5
  21.6 0.7 dynamic_slice.5
  23.0 0.7 dynamic_slice.5
  24.3 0.7 dynamic_slice.5
  25.6 0.7 copy.19
  26.6 0.7 subtract_bitcast_fusion
  27.3 4.0 %collective-permute-start.1 = (s32[32,2]{0,1:T(2,128)S(1)}, s32[32,2]{0,1:T(2,128)S(1)}, u32[]{:S(2)}, u32[]{:S(2)}) collective-permute-start(s32[32,2]{0,1:T(2,128)S(1)} %pad_add_fusion), channel_id=1, source_target_pairs={{1,0},{2,1},{3,2},{4,3},{5,4},{6,5},{7,6},{8,7},{9,8},{10,9},{11,1... | collective-permute-start | bytes 776 | tf_op jit(solution)/shard_map/ppermute | solution.py:17
  31.3 5.3 %collective-permute-start = (s32[32,2]{0,1:T(2,128)S(1)}, s32[32,2]{0,1:T(2,128)S(1)}, u32[]{:S(2)}, u32[]{:S(2)}) collective-permute-start(s32[32,2]{0,1:T(2,128)S(1)} %pad_add_fusion), channel_id=1, source_target_pairs={{0,1},{1,2},{2,3},{3,4},{4,5},{5,6},{6,7},{7,8},{8,9},{9,10},{10,1... | collective-permute-start | bytes 776 | tf_op jit(solution)/shard_map/ppermute | solution.py:14
  36.6 2.4 %collective-permute-start.2 = (bf16[32,512]{1,0:T(8,128)(2,1)}, bf16[32,512]{1,0:T(8,128)(2,1)S(1)}, u32[]{:S(2)}, u32[]{:S(2)}) collective-permute-start(bf16[32,512]{1,0:T(8,128)(2,1)} %param.12), channel_id=1, source_target_pairs={{0,1},{1,2},{2,3},{3,4},{4,5},{5,6},{6,7},{7,8},{8,9},{9,10},{10,1... | collective-permute-start | bytes 98312 | tf_op jit(solution)/shard_map/ppermute | solution.py:14
  39.0 1.9 collective-permute-start.3
  41.1 4.8 %collective-permute-done.3 = bf16[32,512]{1,0:T(8,128)(2,1)S(1)} collective-permute-done((bf16[32,512]{1,0:T(8,128)(2,1)}, bf16[32,512]{1,0:T(8,128)(2,1)S(1)}, u32[]{:S(2)}, u32[]{:S(2)}) %collective-permute-start.3) | collective-permute-done | bytes 32800 | tf_op jit(solution)/shard_map/ppermute | solution.py:17
  45.9 1.5 fusion.34
  47.5 2.0 collective-permute-start.4
  49.5 2.3 %collective-permute-start.5 = (bf16[3,80]{0,1:T(8,128)(2,1)S(1)}, bf16[3,80]{0,1:T(8,128)(2,1)S(1)}, u32[]{:S(2)}, u32[]{:S(2)}) collective-permute-start(bf16[3,80]{0,1:T(8,128)(2,1)S(1)} %get-tuple-element.54), channel_id=1, source_target_pairs={{1,0},{2,1},{3,2},{4,3},{5,4},{6,5},{7,6},{8,7},{9,8},{10,9},{11,1... | collective-permute-start | bytes 1448 | tf_op jit(solution)/shard_map/ppermute | solution.py:17
  51.8 1.3 fusion.105
  53.2 2.3 %collective-permute-done.5 = bf16[3,80]{0,1:T(8,128)(2,1)S(1)} collective-permute-done((bf16[3,80]{0,1:T(8,128)(2,1)S(1)}, bf16[3,80]{0,1:T(8,128)(2,1)S(1)}, u32[]{:S(2)}, u32[]{:S(2)}) %collective-permute-start.5) | collective-permute-done | bytes 512 | tf_op jit(solution)/shard_map/ppermute | solution.py:17
  55.5 1.4 fusion.53
  57.0 0.5 fusion.50
  57.5 0.5 fusion.59
  58.0 0.5 fusion.63
  58.6 0.6 fusion.56
  59.2 1.0 fusion.31
  60.2 2.1 %collective-permute-start.7 = (bf16[1,512]{1,0:T(2,128)(2,1)S(1)}, bf16[1,512]{1,0:T(2,128)(2,1)S(1)}, u32[]{:S(2)}, u32[]{:S(2)}) collective-permute-start(bf16[1,512]{1,0:T(2,128)(2,1)S(1)} %get-tuple-element.51), channel_id=1, source_target_pairs={{1,0},{2,1},{3,2},{4,3},{5,4},{6,5},{7,6},{8,7},{9,8},{10,9},{11,1... | collective-permute-start | bytes 3080 | tf_op jit(solution)/shard_map/ppermute | solution.py:17
  62.2 4.7 %collective-permute-start.6 = (bf16[1,512]{1,0:T(2,128)(2,1)S(1)}, bf16[1,512]{1,0:T(2,128)(2,1)S(1)}, u32[]{:S(2)}, u32[]{:S(2)}) collective-permute-start(bf16[1,512]{1,0:T(2,128)(2,1)S(1)} %get-tuple-element.52), channel_id=1, source_target_pairs={{0,1},{1,2},{2,3},{3,4},{4,5},{5,6},{6,7},{7,8},{8,9},{9,10},{10,1... | collective-permute-start | bytes 3080 | tf_op jit(solution)/shard_map/ppermute | solution.py:14
  67.0 4.2 %copy.24 = bf16[64,8,16,256]{3,1,2,0:T(8,128)(2,1)} copy(bf16[64,8,16,256]{3,2,1,0:T(8,128)(2,1)S(1)} %bitcast.100) | data formatting | bytes 8388608
  71.2 6.5 %copy.21 = bf16[4096,512]{1,0:T(8,128)(2,1)} copy(bf16[4096,512]{0,1:T(8,128)(2,1)} %bitcast.99) | data formatting | bytes 8388608 | tf_op jit(solution)/shard_map/dot_general | solution.py:64
  77.7 1.3 concatenate.57
  79.0 10.4 %fusion.35 = f32[1026,16,256]{2,0,1:T(8,128)} fusion(bf16[16,256,512]{2,1,0:T(8,128)(2,1)} %bitcast.101, bf16[1026,512]{1,0:T(8,128)(2,1)S(1)} %concatenate.57), kind=kOutput, calls=%fused_computation.61 | convolution fusion | flops 4303355904 | bytes 22054912 | tf_op jit(solution)/shard_map/dot_general | solution.py:64
  89.5 9.0 %slice_add_fusion.1 = (f32[1024,4,256]{2,0,1:T(8,128)S(1)}, f32[1024,4,256]{2,0,1:T(8,128)}) fusion(f32[1026,16,256]{2,0,1:T(8,128)} %fusion.35), kind=kLoop, calls=%fused_computation.52 | loop fusion | flops 2097152 | bytes 25165824 | tf_op jit(solution)/shard_map/add | solution.py:70
  98.4 3.5 %fusion.13 = (bf16[1024,8,256]{2,0,1:T(8,128)(2,1)S(1)}, f32[1024,8,256]{2,0,1:T(8,128)S(1)}) fusion(f32[256]{0:T(256)S(1)} %copy-done.5, f32[1024,4,256]{2,0,1:T(8,128)} %get-tuple-element.40, f32[1024,4,256]{2,0,1:T(8,128)S(1)} %get-tuple-element.39), kind=kLoop, calls=%fused_computation.24 | loop fusion | flops 16777216 | bytes 20972544 | tf_op jit(solution)/shard_map/convert_element_type | solution.py:113
  101.9 5.2 %fusion.12 = bf16[8192,256]{1,0:T(8,128)(2,1)S(1)} fusion(f32[256]{0:T(256)S(1)} %copy-done.5, f32[1024,8,256]{2,0,1:T(8,128)S(1)} %get-tuple-element.42), kind=kLoop, calls=%fused_computation.23 | loop fusion | flops 14680064 | bytes 12583936 | tf_op jit(solution)/shard_map/convert_element_type | solution.py:113
  107.1 1.9 collective-permute-start.8
  109.1 2.6 %collective-permute-start.9 = (bf16[1,256]{1,0:T(2,128)(2,1)S(1)}, bf16[1,256]{1,0:T(2,128)(2,1)S(1)}, u32[]{:S(2)}, u32[]{:S(2)}) collective-permute-start(bf16[1,256]{1,0:T(2,128)(2,1)S(1)} %get-tuple-element.50), channel_id=1, source_target_pairs={{1,0},{2,1},{3,2},{4,3},{5,4},{6,5},{7,6},{8,7},{9,8},{10,9},{11,1... | collective-permute-start | bytes 1544 | tf_op jit(solution)/shard_map/ppermute | solution.py:17
  111.7 6.7 %fusion.28 = f32[8192,256]{1,0:T(8,128)} fusion(bf16[1024,8,256]{2,0,1:T(8,128)(2,1)S(1)} %get-tuple-element.41, bf16[4,3,256,256]{3,2,1,0:T(8,128)(2,1)} %param.20), kind=kOutput, calls=%fused_computation.53 | convolution fusion | flops 1073741824 | bytes 12713984 | tf_op jit(solution)/shard_map/dot_general | solution.py:44
  118.4 5.4 %fusion.25 = f32[8192,256]{1,0:T(8,128)} fusion(bf16[1,256]{1,0:T(2,128)(2,1)S(1)} %collective-permute-done.9, bf16[8192,256]{1,0:T(8,128)(2,1)S(1)} %fusion.12, bf16[4,3,256,256]{3,2,1,0:T(8,128)(2,1)} %param.20), kind=kOutput, calls=%fused_computation.47 | convolution fusion | flops 1082130432 | bytes 12714496 | tf_op jit(solution)/shard_map/dot_general | solution.py:44
  123.8 7.4 %fusion.10 = bf16[8192,256]{1,0:T(8,128)(2,1)S(1)} fusion(f32[8192,256]{1,0:T(8,128)} %fusion.25, f32[8192,256]{1,0:T(8,128)} %fusion.28, bf16[8192,256]{1,0:T(8,128)(2,1)S(1)} %fusion.12, bf16[1,256]{1,0:T(2,128)(2,1)S(1)} %collective-permute-done.8, f32[256]{0:T(256)S(1)} %bitcast.105, bf16[4,3,256,256]{3,2,1,0:T(8,128)(2,1)} %param.20), kind=kOutput, calls=%fused_computation.21 | convolution fusion | flops 1096810496 | bytes 25298432 | tf_op jit(solution)/shard_map/dot_general | solution.py:42
  131.3 1.9 collective-permute-start.11
  133.2 5.4 %fusion.74 = f32[8192,256]{1,0:T(8,128)} fusion(bf16[8192,256]{1,0:T(8,128)(2,1)S(1)} %fusion.10, bf16[4,3,256,256]{3,2,1,0:T(8,128)(2,1)} %param.20), kind=kOutput, calls=%fused_computation.100 | convolution fusion | flops 1073741824 | bytes 12713984 | tf_op jit(solution)/shard_map/dot_general | solution.py:44
  138.6 4.5 %collective-permute-start.10 = (bf16[1,256]{1,0:T(2,128)(2,1)S(1)}, bf16[1,256]{1,0:T(2,128)(2,1)S(1)}, u32[]{:S(2)}, u32[]{:S(2)}) collective-permute-start(bf16[1,256]{1,0:T(2,128)(2,1)S(1)} %get-tuple-element.47), channel_id=1, source_target_pairs={{0,1},{1,2},{2,3},{3,4},{4,5},{5,6},{6,7},{7,8},{8,9},{9,10},{10,1... | collective-permute-start | bytes 1544 | tf_op jit(solution)/shard_map/ppermute | solution.py:14
  143.1 5.4 %fusion.22 = f32[8192,256]{1,0:T(8,128)} fusion(bf16[1,256]{1,0:T(2,128)(2,1)S(1)} %collective-permute-done.11, bf16[8192,256]{1,0:T(8,128)(2,1)S(1)} %fusion.10, bf16[4,3,256,256]{3,2,1,0:T(8,128)(2,1)} %param.20), kind=kOutput, calls=%fused_computation.42 | convolution fusion | flops 1082130432 | bytes 12714496 | tf_op jit(solution)/shard_map/dot_general | solution.py:44
  148.6 12.4 %fusion.14 = (bf16[8192,256]{1,0:T(8,128)(2,1)}, bf16[8192,256]{1,0:T(8,128)(2,1)}) fusion(f32[256]{0:T(256)S(1)} %bitcast.104, f32[8192,256]{1,0:T(8,128)} %fusion.22, f32[8192,256]{1,0:T(8,128)} %fusion.74, bf16[4,3,256,256]{3,2,1,0:T(8,128)(2,1)} %param.20, bf16[8192,256]{1,0:T(8,128)(2,1)S(1)} %fusion.10, ...), kind=kOutput, calls=%fused_computation.25 | convolution fusion | flops 1109393408 | bytes 37882368 | tf_op jit(solution)/shard_map/dot_general | solution.py:42
  161.0 0.7 fusion.136
  161.7 1.9 collective-permute-start.12
  163.6 2.7 %collective-permute-start.13 = (bf16[3,256]{1,0:T(4,128)(2,1)S(1)}, bf16[3,256]{1,0:T(4,128)(2,1)S(1)}, u32[]{:S(2)}, u32[]{:S(2)}) collective-permute-start(bf16[3,256]{1,0:T(4,128)(2,1)S(1)} %get-tuple-element.46), channel_id=1, source_target_pairs={{1,0},{2,1},{3,2},{4,3},{5,4},{6,5},{7,6},{8,7},{9,8},{10,9},{11,1... | collective-permute-start | bytes 4616 | tf_op jit(solution)/shard_map/ppermute | solution.py:17
  166.3 7.0 %fusion.70 = f32[8192,256]{1,0:T(8,128)} fusion(bf16[4,3,256,256]{3,2,1,0:T(8,128)(2,1)} %param.20, bf16[8192,256]{1,0:T(8,128)(2,1)} %get-tuple-element.62), kind=kOutput, calls=%fused_computation.96 | convolution fusion | flops 1084227584 | bytes 12713984 | tf_op jit(solution)/shard_map/dot_general | solution.py:44
  173.3 2.2 %fusion.19 = f32[8192,256]{1,0:T(8,128)S(1)} fusion(bf16[3,256]{1,0:T(4,128)(2,1)S(1)} %collective-permute-done.13, bf16[8192,256]{1,0:T(8,128)(2,1)S(1)} %copy-done.2, bf16[4,3,256,256]{3,2,1,0:T(8,128)(2,1)} %param.20), kind=kOutput, calls=%fused_computation.37 | convolution fusion | flops 1082130432 | bytes 12715520 | tf_op jit(solution)/shard_map/dot_general | solution.py:44
  175.5 5.2 %fusion.11 = bf16[8192,256]{1,0:T(8,128)(2,1)S(1)} fusion(f32[8192,256]{1,0:T(8,128)S(1)} %fusion.19, f32[8192,256]{1,0:T(8,128)} %fusion.70, bf16[8192,256]{1,0:T(8,128)(2,1)S(1)} %copy-done.2, bf16[3,256]{1,0:T(4,128)(2,1)S(1)} %collective-permute-done.12, f32[256]{0:T(256)S(1)} %bitcast.103, bf16[4,3,256,256]{3,2,1,0:T(8,128)(2,1)} %param.20), kind=kOutput, calls=%fused_computation.22 | convolution fusion | flops 1096810496 | bytes 25299456 | tf_op jit(solution)/shard_map/dot_general | solution.py:42
  180.7 1.9 collective-permute-start.15
  182.7 5.4 %fusion.66 = f32[8192,256]{1,0:T(8,128)} fusion(bf16[8192,256]{1,0:T(8,128)(2,1)S(1)} %fusion.11, bf16[4,3,256,256]{3,2,1,0:T(8,128)(2,1)} %param.20), kind=kOutput, calls=%fused_computation.92 | convolution fusion | flops 1073741824 | bytes 12713984 | tf_op jit(solution)/shard_map/dot_general | solution.py:44
  188.1 4.5 %collective-permute-start.14 = (bf16[1,256]{1,0:T(2,128)(2,1)S(1)}, bf16[1,256]{1,0:T(2,128)(2,1)S(1)}, u32[]{:S(2)}, u32[]{:S(2)}) collective-permute-start(bf16[1,256]{1,0:T(2,128)(2,1)S(1)} %get-tuple-element.43), channel_id=1, source_target_pairs={{0,1},{1,2},{2,3},{3,4},{4,5},{5,6},{6,7},{7,8},{8,9},{9,10},{10,1... | collective-permute-start | bytes 1544 | tf_op jit(solution)/shard_map/ppermute | solution.py:14
  192.6 2.2 %fusion.16 = f32[8192,256]{1,0:T(8,128)S(1)} fusion(bf16[1,256]{1,0:T(2,128)(2,1)S(1)} %collective-permute-done.15, bf16[8192,256]{1,0:T(8,128)(2,1)S(1)} %fusion.11, bf16[4,3,256,256]{3,2,1,0:T(8,128)(2,1)} %param.20), kind=kOutput, calls=%fused_computation.32 | convolution fusion | flops 1082130432 | bytes 12714496 | tf_op jit(solution)/shard_map/dot_general | solution.py:44
  194.8 7.5 %fusion.9 = bf16[8192,256]{1,0:T(8,128)(2,1)} fusion(f32[8192,256]{1,0:T(8,128)S(1)} %fusion.16, f32[8192,256]{1,0:T(8,128)} %fusion.66, bf16[8192,256]{1,0:T(8,128)(2,1)} %get-tuple-element.62, bf16[8192,256]{1,0:T(8,128)(2,1)S(1)} %fusion.11, bf16[1,256]{1,0:T(2,128)(2,1)S(1)} %collective-permute-done.14, f32[256]{0:T(256)S(1)} %bitcast.102, ...), kind=kOutput, calls=%fused_computation.20 | convolution fusion | flops 1094713344 | bytes 29492736 | tf_op jit(solution)/shard_map/dot_general | solution.py:42
  (44 shorter events, 0.5 us)
Async XLA Ops:
  0.0 45.9 %copy-start = (bf16[512,80]{0,1:T(8,128)(2,1)S(1)}, bf16[512,80]{0,1:T(8,128)(2,1)}, u32[]{:S(2)}) copy-start(bf16[512,80]{0,1:T(8,128)(2,1)} %param.14) | copy-start | bytes 245764
  0.0 56.9 %copy-start.4 = (bf16[7,80,512]{2,1,0:T(8,128)(2,1)S(1)}, bf16[7,80,512]{2,1,0:T(8,128)(2,1)}, u32[]{:S(2)}) copy-start(bf16[7,80,512]{2,1,0:T(8,128)(2,1)} %param.16) | copy-start | bytes 1720324
  27.3 13.7 %collective-permute-start.1 = (s32[32,2]{0,1:T(2,128)S(1)}, s32[32,2]{0,1:T(2,128)S(1)}, u32[]{:S(2)}, u32[]{:S(2)}) collective-permute-start(s32[32,2]{0,1:T(2,128)S(1)} %pad_add_fusion), channel_id=1, source_target_pairs={{1,0},{2,1},{3,2},{4,3},{5,4},{6,5},{7,6},{8,7},{9,8},{10,9},{11,1... | collective-permute-start | bytes 776 | tf_op jit(solution)/shard_map/ppermute | solution.py:17
  31.3 9.7 %collective-permute-start = (s32[32,2]{0,1:T(2,128)S(1)}, s32[32,2]{0,1:T(2,128)S(1)}, u32[]{:S(2)}, u32[]{:S(2)}) collective-permute-start(s32[32,2]{0,1:T(2,128)S(1)} %pad_add_fusion), channel_id=1, source_target_pairs={{0,1},{1,2},{2,3},{3,4},{4,5},{5,6},{6,7},{7,8},{8,9},{9,10},{10,1... | collective-permute-start | bytes 776 | tf_op jit(solution)/shard_map/ppermute | solution.py:14
  36.6 4.5 %collective-permute-start.2 = (bf16[32,512]{1,0:T(8,128)(2,1)}, bf16[32,512]{1,0:T(8,128)(2,1)S(1)}, u32[]{:S(2)}, u32[]{:S(2)}) collective-permute-start(bf16[32,512]{1,0:T(8,128)(2,1)} %param.12), channel_id=1, source_target_pairs={{0,1},{1,2},{2,3},{3,4},{4,5},{5,6},{6,7},{7,8},{8,9},{9,10},{10,1... | collective-permute-start | bytes 98312 | tf_op jit(solution)/shard_map/ppermute | solution.py:14
  39.0 6.9 %collective-permute-start.3 = (bf16[32,512]{1,0:T(8,128)(2,1)}, bf16[32,512]{1,0:T(8,128)(2,1)S(1)}, u32[]{:S(2)}, u32[]{:S(2)}) collective-permute-start(bf16[32,512]{1,0:T(8,128)(2,1)} %param.12), channel_id=1, source_target_pairs={{1,0},{2,1},{3,2},{4,3},{5,4},{6,5},{7,6},{8,7},{9,8},{10,9},{11,1... | collective-permute-start | bytes 98312 | tf_op jit(solution)/shard_map/ppermute | solution.py:17
  47.5 10.0 %collective-permute-start.4 = (bf16[3,80]{0,1:T(8,128)(2,1)S(1)}, bf16[3,80]{0,1:T(8,128)(2,1)S(1)}, u32[]{:S(2)}, u32[]{:S(2)}) collective-permute-start(bf16[3,80]{0,1:T(8,128)(2,1)S(1)} %get-tuple-element.53), channel_id=1, source_target_pairs={{0,1},{1,2},{2,3},{3,4},{4,5},{5,6},{6,7},{7,8},{8,9},{9,10},{10,1... | collective-permute-start | bytes 1448 | tf_op jit(solution)/shard_map/ppermute | solution.py:14
  49.5 6.0 %collective-permute-start.5 = (bf16[3,80]{0,1:T(8,128)(2,1)S(1)}, bf16[3,80]{0,1:T(8,128)(2,1)S(1)}, u32[]{:S(2)}, u32[]{:S(2)}) collective-permute-start(bf16[3,80]{0,1:T(8,128)(2,1)S(1)} %get-tuple-element.54), channel_id=1, source_target_pairs={{1,0},{2,1},{3,2},{4,3},{5,4},{6,5},{7,6},{8,7},{9,8},{10,9},{11,1... | collective-permute-start | bytes 1448 | tf_op jit(solution)/shard_map/ppermute | solution.py:17
  56.9 2.2 %copy-start.7 = (f32[512]{0:T(512)S(1)}, f32[512]{0:T(512)}, u32[]{:S(2)}) copy-start(f32[512]{0:T(512)} %param.17) | copy-start | bytes 6148
  59.1 7.8 %copy-start.6 = (f32[4,256]{1,0:T(4,128)S(1)}, f32[4,256]{1,0:T(4,128)}, u32[]{:S(2)}) copy-start(f32[4,256]{1,0:T(4,128)} %param.21) | copy-start | bytes 12292
  59.2 7.8 %copy-start.3 = (bf16[512,16,256]{2,1,0:T(8,128)(2,1)S(1)}, bf16[512,16,256]{2,1,0:T(8,128)(2,1)}, u32[]{:S(2)}) copy-start(bf16[512,16,256]{2,1,0:T(8,128)(2,1)} %param.18) | copy-start | bytes 12582916
  60.2 17.6 %collective-permute-start.7 = (bf16[1,512]{1,0:T(2,128)(2,1)S(1)}, bf16[1,512]{1,0:T(2,128)(2,1)S(1)}, u32[]{:S(2)}, u32[]{:S(2)}) collective-permute-start(bf16[1,512]{1,0:T(2,128)(2,1)S(1)} %get-tuple-element.51), channel_id=1, source_target_pairs={{1,0},{2,1},{3,2},{4,3},{5,4},{6,5},{7,6},{8,7},{9,8},{10,9},{11,1... | collective-permute-start | bytes 3080 | tf_op jit(solution)/shard_map/ppermute | solution.py:17
  62.2 15.5 %collective-permute-start.6 = (bf16[1,512]{1,0:T(2,128)(2,1)S(1)}, bf16[1,512]{1,0:T(2,128)(2,1)S(1)}, u32[]{:S(2)}, u32[]{:S(2)}) collective-permute-start(bf16[1,512]{1,0:T(2,128)(2,1)S(1)} %get-tuple-element.52), channel_id=1, source_target_pairs={{0,1},{1,2},{2,3},{3,4},{4,5},{5,6},{6,7},{7,8},{8,9},{9,10},{10,1... | collective-permute-start | bytes 3080 | tf_op jit(solution)/shard_map/ppermute | solution.py:14
  89.5 9.0 %copy-start.5 = (f32[256]{0:T(256)S(1)}, f32[256]{0:T(256)}, u32[]{:S(2)}) copy-start(f32[256]{0:T(256)} %param.19) | copy-start | bytes 3076
  107.1 16.7 %collective-permute-start.8 = (bf16[1,256]{1,0:T(2,128)(2,1)S(1)}, bf16[1,256]{1,0:T(2,128)(2,1)S(1)}, u32[]{:S(2)}, u32[]{:S(2)}) collective-permute-start(bf16[1,256]{1,0:T(2,128)(2,1)S(1)} %get-tuple-element.49), channel_id=1, source_target_pairs={{0,1},{1,2},{2,3},{3,4},{4,5},{5,6},{6,7},{7,8},{8,9},{9,10},{10,1... | collective-permute-start | bytes 1544 | tf_op jit(solution)/shard_map/ppermute | solution.py:14
  109.1 9.3 %collective-permute-start.9 = (bf16[1,256]{1,0:T(2,128)(2,1)S(1)}, bf16[1,256]{1,0:T(2,128)(2,1)S(1)}, u32[]{:S(2)}, u32[]{:S(2)}) collective-permute-start(bf16[1,256]{1,0:T(2,128)(2,1)S(1)} %get-tuple-element.50), channel_id=1, source_target_pairs={{1,0},{2,1},{3,2},{4,3},{5,4},{6,5},{7,6},{8,7},{9,8},{10,9},{11,1... | collective-permute-start | bytes 1544 | tf_op jit(solution)/shard_map/ppermute | solution.py:17
  131.3 11.9 %collective-permute-start.11 = (bf16[1,256]{1,0:T(2,128)(2,1)S(1)}, bf16[1,256]{1,0:T(2,128)(2,1)S(1)}, u32[]{:S(2)}, u32[]{:S(2)}) collective-permute-start(bf16[1,256]{1,0:T(2,128)(2,1)S(1)} %get-tuple-element.48), channel_id=1, source_target_pairs={{1,0},{2,1},{3,2},{4,3},{5,4},{6,5},{7,6},{8,7},{9,8},{10,9},{11,1... | collective-permute-start | bytes 1544 | tf_op jit(solution)/shard_map/ppermute | solution.py:17
  138.6 10.0 %collective-permute-start.10 = (bf16[1,256]{1,0:T(2,128)(2,1)S(1)}, bf16[1,256]{1,0:T(2,128)(2,1)S(1)}, u32[]{:S(2)}, u32[]{:S(2)}) collective-permute-start(bf16[1,256]{1,0:T(2,128)(2,1)S(1)} %get-tuple-element.47), channel_id=1, source_target_pairs={{0,1},{1,2},{2,3},{3,4},{4,5},{5,6},{6,7},{7,8},{8,9},{9,10},{10,1... | collective-permute-start | bytes 1544 | tf_op jit(solution)/shard_map/ppermute | solution.py:14
  161.7 13.8 %collective-permute-start.12 = (bf16[3,256]{1,0:T(4,128)(2,1)S(1)}, bf16[3,256]{1,0:T(4,128)(2,1)S(1)}, u32[]{:S(2)}, u32[]{:S(2)}) collective-permute-start(bf16[3,256]{1,0:T(4,128)(2,1)S(1)} %get-tuple-element.45), channel_id=1, source_target_pairs={{0,1},{1,2},{2,3},{3,4},{4,5},{5,6},{6,7},{7,8},{8,9},{9,10},{10,1... | collective-permute-start | bytes 4616 | tf_op jit(solution)/shard_map/ppermute | solution.py:14
  163.6 9.7 %collective-permute-start.13 = (bf16[3,256]{1,0:T(4,128)(2,1)S(1)}, bf16[3,256]{1,0:T(4,128)(2,1)S(1)}, u32[]{:S(2)}, u32[]{:S(2)}) collective-permute-start(bf16[3,256]{1,0:T(4,128)(2,1)S(1)} %get-tuple-element.46), channel_id=1, source_target_pairs={{1,0},{2,1},{3,2},{4,3},{5,4},{6,5},{7,6},{8,7},{9,8},{10,9},{11,1... | collective-permute-start | bytes 4616 | tf_op jit(solution)/shard_map/ppermute | solution.py:17
  166.3 7.0 %copy-start.2 = (bf16[8192,256]{1,0:T(8,128)(2,1)S(1)}, bf16[8192,256]{1,0:T(8,128)(2,1)}, u32[]{:S(2)}) copy-start(bf16[8192,256]{1,0:T(8,128)(2,1)} %get-tuple-element.61) | copy-start | bytes 12582916
  180.7 11.9 %collective-permute-start.15 = (bf16[1,256]{1,0:T(2,128)(2,1)S(1)}, bf16[1,256]{1,0:T(2,128)(2,1)S(1)}, u32[]{:S(2)}, u32[]{:S(2)}) collective-permute-start(bf16[1,256]{1,0:T(2,128)(2,1)S(1)} %get-tuple-element.44), channel_id=1, source_target_pairs={{1,0},{2,1},{3,2},{4,3},{5,4},{6,5},{7,6},{8,7},{9,8},{10,9},{11,1... | collective-permute-start | bytes 1544 | tf_op jit(solution)/shard_map/ppermute | solution.py:17
  188.1 6.7 %collective-permute-start.14 = (bf16[1,256]{1,0:T(2,128)(2,1)S(1)}, bf16[1,256]{1,0:T(2,128)(2,1)S(1)}, u32[]{:S(2)}, u32[]{:S(2)}) collective-permute-start(bf16[1,256]{1,0:T(2,128)(2,1)S(1)} %get-tuple-element.43), channel_id=1, source_target_pairs={{0,1},{1,2},{2,3},{3,4},{4,5},{5,6},{6,7},{7,8},{8,9},{9,10},{10,1... | collective-permute-start | bytes 1544 | tf_op jit(solution)/shard_map/ppermute | solution.py:14
  194.8 7.5 %copy-start.1 = (bf16[512,80]{0,1:T(8,128)(2,1)S(1)}, bf16[512,80]{0,1:T(8,128)(2,1)}, u32[]{:S(2)}) copy-start(bf16[512,80]{0,1:T(8,128)(2,1)} %param.14) | copy-start | bytes 245764
where the time goes:
time: 203 us; the launch traced here: 202 us
  matrix products  90 us (44%)
  starting transfers between devices  46.7 us (23%)
  local copies, waits for them, and re-layouts  23.6 us (12%)
  other arithmetic  20 us (10%)
  loops' own time  7.67 us (4%)
  waiting for transfers between devices  7.2 us (4%)
  blocking collectives  6.6 us (3%)
    dot_general x14, matrix products, tap_sum(): jnp.dot(padded[k * dilation:k * dilation + length], weight[k], preferred_...  45.1 us
    dot_general x5, matrix products, tap_sum(): jnp.dot(padded[0:length], weight[0], preferred_element_type=jnp.float32)  33 us
    ppermute x8, starting transfers between devices, with_halo(): lax.ppermute(lax.slice_in_dim(block, block.shape[dim] - width, None, axis...  27.3 us
    ppermute x8, starting transfers between devices, with_halo(): lax.ppermute(lax.slice_in_dim(block, 0, width, axis=dim), axis, backward)  19.4 us
    dot_general x1, matrix products, upsample(): jnp.dot(act_rows, up_weight.reshape(channels_in, taps_count * channels_ou...  10.4 us
    add x1, other arithmetic, upsample(): lower = taps[1:count + 1, 4:8] + taps[0:count, 12:16]  8.99 us
    convert_element_type x2, other arithmetic, on_device(): inner = leaky(state.astype(jnp.float32)).astype(jnp.bfloat16)  8.65 us
    another operation x1, loops' own time, entering(): return lax.fori_loop(0, place, one, state)  7.67 us
  transfers between devices with their start and end apart: 16, of which 2 were waited for; matrix products, arithmetic and copies ran while one was open for 27% of the time, Pallas kernels for 0%

commit v1 on v0

v1 whole, which is shorter than its diff:
```python
import functools

import jax
import jax.numpy as jnp
from jax import lax
from jax.experimental import pallas as pl
from jax.experimental.pallas import tpu as pltpu
from jax.sharding import PartitionSpec as P

LANES = 128
TAPS = 16
PAD = 8
HALO = 16
MIB = 1024 * 1024


def leaky(v):
    return jnp.maximum(v, 0.1 * v)


def gather_kernel(
    count,
    dur_ref,
    hidden_ref,
    mel_w_ref,
    mel_b_ref,
    pre_w_hbm,
    up_w_hbm,
    mel_out,
    dur_out,
    pre_out,
    up_out,
    mel_own,
    mel_low,
    mel_high,
    dur_all,
    dur_own,
    pre_w,
    up_w,
    spread,
    load_sem,
    send_dur,
    recv_dur,
    send_mel,
    recv_mel,
):
    me = lax.axis_index("tm")
    load_pre = pltpu.make_async_copy(pre_w_hbm, pre_w, load_sem.at[0])
    load_up = pltpu.make_async_copy(up_w_hbm, up_w, load_sem.at[1])
    load_up.start()
    load_pre.start()
    barrier = pltpu.get_barrier_semaphore()
    for d in range(1, count):
        pl.semaphore_signal(
            barrier,
            inc=1,
            device_id={"tm": lax.rem(me + d, count)},
            device_id_type=pl.DeviceIdType.MESH,
        )
    phonemes = hidden_ref.shape[0]
    channels = mel_w_ref.shape[1]
    dur_own[...] = jnp.zeros_like(dur_own)
    dur_own[0:1, 0:phonemes] = dur_ref[...]
    mel = jnp.dot(hidden_ref[...], mel_w_ref[...], preferred_element_type=jnp.float32)
    mel = (mel + mel_b_ref[...]).astype(jnp.bfloat16)
    mel_own[...] = jnp.zeros_like(mel_own)
    mel_own[:, 0:channels] = mel
    pl.semaphore_wait(barrier, count - 1)

    copies = []
    for side, (hop, landing) in enumerate(((1, mel_low), (count - 1, mel_high))):
        copies.append(
            pltpu.make_async_remote_copy(
                src_ref=mel_own,
                dst_ref=landing,
                send_sem=send_mel.at[side],
                recv_sem=recv_mel.at[side],
                device_id={"tm": lax.rem(me + hop, count)},
                device_id_type=pl.DeviceIdType.MESH,
            )
        )
    for d in range(1, count):
        copies.append(
            pltpu.make_async_remote_copy(
                src_ref=dur_own,
                dst_ref=dur_all.at[d],
                send_sem=send_dur.at[d],
                recv_sem=recv_dur.at[d],
                device_id={"tm": lax.rem(me + d, count)},
                device_id_type=pl.DeviceIdType.MESH,
            )
        )
    for copy in copies:
        copy.start()

    load_pre.wait()
    pre_out[...] = jnp.zeros_like(pre_out)
    for k in range(pre_w.shape[0]):
        pre_out[k * LANES : k * LANES + channels, :] = pre_w[k]

    load_up.wait()
    step = 32
    width = up_w.shape[2]

    def relay(i, carry):
        first = pl.multiple_of(i * step, step)
        block = up_w[pl.ds(first, step)].reshape(step * TAPS, width).astype(jnp.float32)
        for h in range(width // LANES):
            spread[h] = block[:, h * LANES : (h + 1) * LANES]
        for k in range(TAPS):
            for h in range(width // LANES):
                part = spread[h, pl.ds(k, step, stride=TAPS), :]
                up_out[k, pl.ds(first, step), h * LANES : (h + 1) * LANES] = part.astype(jnp.bfloat16)
        return carry

    lax.fori_loop(0, up_w.shape[0] // step, relay, 0)

    for copy in copies:
        copy.wait()
    mel_out[...] = jnp.zeros_like(mel_out)
    mel_out[0:phonemes, :] = mel_low[...]
    mel_out[LANES : LANES + phonemes, :] = mel_own[...]
    mel_out[2 * LANES : 2 * LANES + phonemes, :] = mel_high[...]
    dur_out[0] = dur_own[...]
    for d in range(1, count):
        dur_out[d] = dur_all[d]


def main_kernel(
    count,
    frames,
    chunk,
    mel_ref,
    dur_ref,
    pre_w,
    pre_b,
    up_hbm,
    up_b,
    res_hbm,
    res_b,
    out_hbm,
    up_w,
    res_w,
    mel32,
    act32,
    x,
    xt,
    c,
    xt_sh,
    c_sh,
    weave,
    out_v,
    load_sem,
    out_sem,
):
    bf = jnp.bfloat16
    f32 = jnp.float32
    rows = frames + 2 * HALO
    me = lax.axis_index("tm")
    load_up = pltpu.make_async_copy(up_hbm, up_w, load_sem.at[0])
    load_res = pltpu.make_async_copy(res_hbm, res_w, load_sem.at[1])
    load_up.start()
    load_res.start()
    inside_low = me > 0
    inside_high = me < count - 1

    def edges(value, first):
        parts = []
        low, high = 0, value.shape[0]
        if first == 0:
            parts.append(jnp.where(inside_low, value[:HALO], 0.0))
            low = HALO
        if first + value.shape[0] == rows:
            high -= HALO
        parts.append(value[low:high])
        if first + value.shape[0] == rows:
            parts.append(jnp.where(inside_high, value[high:], 0.0))
        return jnp.concatenate(parts, axis=0) if len(parts) > 1 else value

    chunks = [(r, chunk) for r in range(0, rows, chunk)]

    durations = dur_ref[...].astype(f32)
    slot = lax.broadcasted_iota(jnp.int32, durations.shape, 0)
    lane_a = lax.broadcasted_iota(jnp.int32, (LANES, LANES), 0)
    lane_b = lax.broadcasted_iota(jnp.int32, (LANES, LANES), 1)
    before = jnp.where(lane_a < lane_b, 1.0, 0.0).astype(bf)
    earlier = jnp.sum(jnp.where((slot >= 1) & (slot <= me), durations, 0.0), axis=0)
    offset = jnp.sum(earlier, axis=(0, 1), keepdims=True)
    own = dur_ref[0].astype(f32)
    low = dur_ref[1].astype(f32)
    high = dur_ref[count - 1].astype(f32)
    total_own = jnp.sum(own, axis=(0, 1), keepdims=True)
    total_low = jnp.sum(low, axis=(0, 1), keepdims=True)
    bounds = []
    for tile, base, valid in (
        (low, offset - total_low, inside_low),
        (own, offset, None),
        (high, offset + total_own, inside_high),
    ):
        if valid is not None:
            tile = jnp.where(valid, tile, 0.0)
        start = (base + jnp.dot(tile.astype(bf), before, preferred_element_type=f32))[0:1]
        bounds.append((start, start + tile[0:1]))
    first_frame = me * frames - HALO
    for r, n in chunks:
        ids = (lax.broadcasted_iota(jnp.int32, (n, LANES), 0) + (first_frame + r)).astype(f32)
        hot = jnp.concatenate(
            [jnp.where((ids >= s) & (ids < e), 1.0, 0.0).astype(bf) for s, e in bounds], axis=1
        )
        mel32[PAD + r : PAD + r + n, :] = jnp.dot(hot, mel_ref[...], preferred_element_type=f32)

    for r, n in chunks:
        taps = jnp.concatenate(
            [mel32[PAD + r + k - 3 : PAD + r + k - 3 + n, :].astype(bf) for k in range(7)], axis=1
        )
        pre = jnp.dot(taps, pre_w[...], preferred_element_type=f32) + pre_b[...]
        act32[PAD + r : PAD + r + n, :] = edges(leaky(pre), r)

    def put_xt(value, p, r, n, dil):
        v = leaky(value.astype(f32))
        xt[p, r : r + n, :] = v.astype(bf)
        if p < dil:
            xt_sh[p, PAD + r : PAD + r + n, :] = edges(v, r)
        if p >= 8 - dil:
            xt_sh[p - 2, PAD + r : PAD + r + n, :] = edges(v, r)

    load_up.wait()
    for r, n in chunks:
        here = act32[PAD + r : PAD + r + n, :].astype(bf)
        prior = act32[PAD + r - 1 : PAD + r - 1 + n, :].astype(bf)
        after = act32[PAD + r + 1 : PAD + r + 1 + n, :].astype(bf)
        for p in range(8):
            other, tap = (prior, p + 12) if p < 4 else (after, p - 4)
            lhs = jnp.concatenate([here, other], axis=1)
            rhs = jnp.concatenate([up_w[p + 4], up_w[tap]], axis=0)
            value = (jnp.dot(lhs, rhs, preferred_element_type=f32) + up_b[...]).astype(bf)
            x[p, r : r + n, :] = value
            put_xt(value, p, r, n, 1)

    def gathered(main, shifted, index, p, dil, r, n):
        parts = []
        for k in (-1, 0, 1):
            q = p + k * dil
            if q < 0:
                parts.append(shifted[index(q + 8), PAD + r - 1 : PAD + r - 1 + n, :].astype(bf))
            elif q > 7:
                parts.append(shifted[index(q - 8), PAD + r + 1 : PAD + r + 1 + n, :].astype(bf))
            else:
                parts.append(main[q, r : r + n, :])
        return jnp.concatenate(parts, axis=1)

    def xt_index(q):
        return q if q < 3 else q - 2

    def c_index(q):
        return 0 if q == 0 else 1

    def weight(j):
        return res_w[j].reshape(3 * res_w.shape[2], res_w.shape[3])

    def inner(j, dil):
        for r, n in chunks:
            for p in range(8):
                lhs = gathered(xt, xt_sh, xt_index, p, dil, r, n)
                v = jnp.dot(lhs, weight(j), preferred_element_type=f32) + res_b[j : j + 1]
                v = leaky(v)
                c[p, r : r + n, :] = v.astype(bf)
                if p in (0, 7):
                    c_sh[c_index(p), PAD + r : PAD + r + n, :] = edges(v, r)

    load_res.wait()
    inner(0, 1)
    for r, n in chunks:
        for p in range(8):
            lhs = gathered(c, c_sh, c_index, p, 1, r, n)
            v = jnp.dot(lhs, weight(1), preferred_element_type=f32) + res_b[1:2]
            value = (x[p, r : r + n, :].astype(f32) + v).astype(bf)
            x[p, r : r + n, :] = value
            put_xt(value, p, r, n, 3)
    inner(2, 3)
    n = frames // 4
    stores = []
    for i in range(4):
        r = HALO + i * n
        for p in range(8):
            lhs = gathered(c, c_sh, c_index, p, 1, r, n)
            v = jnp.dot(lhs, weight(3), preferred_element_type=f32) + res_b[3:4]
            v = x[p, r : r + n, :].astype(f32) + v
            for h in range(2):
                weave[i % 2, h, pl.ds(p, n, stride=8), :] = v[:, h * LANES : (h + 1) * LANES]
        for h in range(2):
            out_v[i * n * 8 : (i + 1) * n * 8, h * LANES : (h + 1) * LANES] = weave[i % 2, h].astype(bf)
        store = pltpu.make_async_copy(
            out_v.at[pl.ds(i * n * 8, n * 8)], out_hbm.at[pl.ds(i * n * 8, n * 8)], out_sem.at[i]
        )
        store.start()
        stores.append(store)
    for store in stores:
        store.wait()


def on_device(
    frames,
    count,
    hidden,
    durations,
    mel_weight,
    mel_bias,
    pre_weight,
    pre_bias,
    up_weight,
    up_bias,
    res_weight,
    res_bias,
):
    phonemes, _ = hidden.shape
    taps, channels, inner = pre_weight.shape
    width = up_weight.shape[2]
    bf, f32, i32 = jnp.bfloat16, jnp.float32, jnp.int32
    vmem = pl.BlockSpec(memory_space=pltpu.VMEM)
    hbm = pl.BlockSpec(memory_space=pl.ANY)
    dma = pltpu.SemaphoreType.DMA
    mel_near, dur_all, pre_w, up_w = pl.pallas_call(
        functools.partial(gather_kernel, count),
        out_shape=(
            jax.ShapeDtypeStruct((3 * LANES, LANES), bf),
            jax.ShapeDtypeStruct((count, 8, LANES), i32),
            jax.ShapeDtypeStruct((taps * LANES, inner), bf),
            jax.ShapeDtypeStruct((TAPS, inner, width), bf),
        ),
        in_specs=[vmem, vmem, vmem, vmem, hbm, hbm],
        out_specs=(vmem, vmem, vmem, vmem),
        scratch_shapes=[
            pltpu.VMEM((phonemes, LANES), bf),
            pltpu.VMEM((phonemes, LANES), bf),
            pltpu.VMEM((phonemes, LANES), bf),
            pltpu.VMEM((count, 8, LANES), i32),
            pltpu.VMEM((8, LANES), i32),
            pltpu.VMEM(pre_weight.shape, bf),
            pltpu.VMEM(up_weight.shape, bf),
            pltpu.VMEM((2, 32 * TAPS, LANES), f32),
            dma((2,)),
            dma((count,)),
            dma((count,)),
            dma((2,)),
            dma((2,)),
        ],
        compiler_params=pltpu.CompilerParams(
            collective_id=0, has_side_effects=True, vmem_limit_bytes=24 * MIB
        ),
        name="gather_states",
    )(durations.reshape(1, -1), hidden, mel_weight, mel_bias.reshape(1, -1), pre_weight, up_weight)

    rows = frames + 2 * HALO
    chunk = rows // 3
    return pl.pallas_call(
        functools.partial(main_kernel, count, frames, chunk),
        out_shape=jax.ShapeDtypeStruct((frames * 8, width), bf),
        in_specs=[vmem, vmem, vmem, vmem, hbm, vmem, hbm, vmem],
        out_specs=hbm,
        scratch_shapes=[
            pltpu.VMEM(up_w.shape, bf),
            pltpu.VMEM(res_weight.shape, bf),
            pltpu.VMEM((rows + 2 * PAD, LANES), f32),
            pltpu.VMEM((rows + 2 * PAD, inner), f32),
            pltpu.VMEM((8, rows, width), bf),
            pltpu.VMEM((8, rows, width), bf),
            pltpu.VMEM((8, rows, width), bf),
            pltpu.VMEM((6, rows + 2 * PAD, width), f32),
            pltpu.VMEM((2, rows + 2 * PAD, width), f32),
            pltpu.VMEM((2, 2, frames * 2, LANES), f32),
            pltpu.VMEM((frames * 8, width), bf),
            dma((2,)),
            dma((4,)),
        ],
        compiler_params=pltpu.CompilerParams(vmem_limit_bytes=56 * MIB),
        name="vocoder_section",
    )(
        mel_near,
        dur_all,
        pre_w,
        pre_bias.reshape(1, -1),
        up_w,
        up_bias.reshape(1, -1),
        res_weight,
        res_bias,
    )


def solution(mesh):
    count = mesh.shape["tm"]

    def run(hidden, durations, *weights):
        frames = 32 * hidden.shape[0]
        return on_device(frames, count, hidden, durations, *weights)

    both = ("groups", "tm")
    in_specs = (P(both, None), P(both)) + (P(),) * 8
    return jax.shard_map(
        run, mesh=mesh, in_specs=in_specs, out_specs=P(both, None), check_vma=False
    )
```

time: 203 us -> 45.7 us (0.23)
  the two profiles are of different devices: /device:TPU:21 before, /device:TPU:0 now
where the time goes in v1:
time: 45.7 us; the launch traced here: 45.4 us
  Pallas kernels  34.8 us (76%)
  local copies, waits for them, and re-layouts  10.4 us (23%)
    pallas_call x1, Pallas kernels, on_device(): pl.pallas_call(functools.partial(main_kernel, count, frames, chunk), out_...  24.5 us
    unnamed x19, local copies, waits for them, and re-layouts  10.4 us
    pallas_call x1, Pallas kernels, on_device(): pl.pallas_call(functools.partial(gather_kernel, count), out_shape=(jax.Sh...  10.3 us

profile of v1, /device:TPU:0, one launch (start us, length us, event | category | flops | bytes accessed | tf_op | source)
XLA Modules:
  0.0 45.4 jit_solution(2668331187858923834)
XLA Ops:
  0.0 1.0 %copy.11.mel_w_ref = bf16[512,80]{1,0:T(8,128)(2,1)S(1)} copy(bf16[512,80]{0,1:T(8,128)(2,1)} %param.12) | data formatting | bytes 163840 | tf_op args[2]
  1.0 0.0 copy-start
  1.0 2.2 %copy-done = bf16[512,16,256]{2,1,0:T(8,128)(2,1)S(1)} copy-done((bf16[512,16,256]{2,1,0:T(8,128)(2,1)S(1)}, bf16[512,16,256]{2,1,0:T(8,128)(2,1)}, u32[]{:S(2)}) %copy-start) | copy-done | bytes 4194328
  3.2 0.0 copy-start.3
  3.2 1.1 %copy-done.3 = bf16[7,80,512]{2,1,0:T(8,128)(2,1)S(1)} copy-done((bf16[7,80,512]{2,1,0:T(8,128)(2,1)S(1)}, bf16[7,80,512]{2,1,0:T(8,128)(2,1)}, u32[]{:S(2)}) %copy-start.3) | copy-done | bytes 573464
  4.3 0.0 copy-start.6
  4.3 0.8 %copy-done.6 = bf16[32,512]{1,0:T(8,128)(2,1)S(1)} copy-done((bf16[32,512]{1,0:T(8,128)(2,1)S(1)}, bf16[32,512]{1,0:T(8,128)(2,1)}, u32[]{:S(2)}) %copy-start.6) | copy-done | bytes 32792
  5.0 0.0 copy-start.7
  5.0 0.7 %copy-done.7 = s32[32]{0:T(128)S(1)} copy-done((s32[32]{0:T(128)S(1)}, s32[32]{0:T(128)}, u32[]{:S(2)}) %copy-start.7) | copy-done | bytes 152
  5.7 0.0 copy-start.8
  5.7 0.7 %copy-done.8 = f32[80]{0:T(128)S(1)} copy-done((f32[80]{0:T(128)S(1)}, f32[80]{0:T(128)}, u32[]{:S(2)}) %copy-start.8) | copy-done | bytes 344
  6.3 10.3 %gather_states.1 = (bf16[384,128]{1,0:T(8,128)(2,1)S(1)}, s32[16,8,128]{2,1,0:T(8,128)S(1)}, bf16[896,512]{1,0:T(8,128)(2,1)S(1)}, bf16[16,512,256]{2,1,0:T(8,128)(2,1)S(1)}) custom-call(s32[1,32]{1,0:T(1,128)S(1)} %bitcast.4, bf16[32,512]{1,0:T(8,128)(2,1)S(1)} %copy-done.6, bf16[512,80]{1,0:T(8,128)(2,1)S(1)} %copy.11.mel_w_ref, f32[1,80]{1,0:T(1,128)S(1)} %bitcast.5, ...), custom_call_target="tpu_custom_call" | custom-call | tf_op jit(solution)/shard_map/gather_states/pallas_call | solution.py:323
  16.6 0.0 copy-start.1
  16.6 1.9 %copy-done.1 = bf16[16,512,256]{2,1,0:T(8,128)(2,1)} copy-done((bf16[16,512,256]{2,1,0:T(8,128)(2,1)}, bf16[16,512,256]{2,1,0:T(8,128)(2,1)S(1)}, u32[]{:S(2)}) %copy-start.1) | copy-done | bytes 4194328
  18.6 0.0 copy-start.2
  18.6 0.9 %copy-done.2 = bf16[896,512]{1,0:T(8,128)(2,1)} copy-done((bf16[896,512]{1,0:T(8,128)(2,1)}, bf16[896,512]{1,0:T(8,128)(2,1)S(1)}, u32[]{:S(2)}) %copy-start.2) | copy-done | bytes 917528
  19.5 0.0 copy-start.4
  19.5 0.6 %copy-done.4 = bf16[384,128]{1,0:T(8,128)(2,1)} copy-done((bf16[384,128]{1,0:T(8,128)(2,1)}, bf16[384,128]{1,0:T(8,128)(2,1)S(1)}, u32[]{:S(2)}) %copy-start.4) | copy-done | bytes 98328
  20.1 0.0 copy-start.5
  20.1 0.6 %copy-done.5 = s32[16,8,128]{2,1,0:T(8,128)} copy-done((s32[16,8,128]{2,1,0:T(8,128)}, s32[16,8,128]{2,1,0:T(8,128)S(1)}, u32[]{:S(2)}) %copy-start.5) | copy-done | bytes 65560
  20.7 24.5 %vocoder_section.1 = bf16[8192,256]{1,0:T(8,128)(2,1)} custom-call(bf16[384,128]{1,0:T(8,128)(2,1)} %copy-done.4, s32[16,8,128]{2,1,0:T(8,128)} %copy-done.5, bf16[896,512]{1,0:T(8,128)(2,1)} %copy-done.2, f32[1,512]{1,0:T(1,128)} %bitcast.6, bf16[16,512,256]{2,1,0:T(8,128)(2,1)} %copy-done.1, f32[1,256]{1,0:T(1,128)} %bitcast.7, ...), custom_call_target="tpu_custom_call" | custom-call | tf_op jit(solution)/shard_map/vocoder_section/pallas_call | solution.py:356
Async XLA Ops:
  1.0 2.2 %copy-start = (bf16[512,16,256]{2,1,0:T(8,128)(2,1)S(1)}, bf16[512,16,256]{2,1,0:T(8,128)(2,1)}, u32[]{:S(2)}) copy-start(bf16[512,16,256]{2,1,0:T(8,128)(2,1)} %up_w_hbm.1) | copy-start | bytes 12582916
  3.2 1.1 %copy-start.3 = (bf16[7,80,512]{2,1,0:T(8,128)(2,1)S(1)}, bf16[7,80,512]{2,1,0:T(8,128)(2,1)}, u32[]{:S(2)}) copy-start(bf16[7,80,512]{2,1,0:T(8,128)(2,1)} %pre_w_hbm.1) | copy-start | bytes 1720324
  4.3 0.8 %copy-start.6 = (bf16[32,512]{1,0:T(8,128)(2,1)S(1)}, bf16[32,512]{1,0:T(8,128)(2,1)}, u32[]{:S(2)}) copy-start(bf16[32,512]{1,0:T(8,128)(2,1)} %hidden_ref.1) | copy-start | bytes 98308
  5.0 0.7 %copy-start.7 = (s32[32]{0:T(128)S(1)}, s32[32]{0:T(128)}, u32[]{:S(2)}) copy-start(s32[32]{0:T(128)} %param.11) | copy-start | bytes 388
  5.7 0.7 %copy-start.8 = (f32[80]{0:T(128)S(1)}, f32[80]{0:T(128)}, u32[]{:S(2)}) copy-start(f32[80]{0:T(128)} %param.13) | copy-start | bytes 964
  16.6 1.9 %copy-start.1 = (bf16[16,512,256]{2,1,0:T(8,128)(2,1)}, bf16[16,512,256]{2,1,0:T(8,128)(2,1)S(1)}, u32[]{:S(2)}) copy-start(bf16[16,512,256]{2,1,0:T(8,128)(2,1)S(1)} %get-tuple-element.12.up_hbm) | copy-start | bytes 12582916
  18.6 0.9 %copy-start.2 = (bf16[896,512]{1,0:T(8,128)(2,1)}, bf16[896,512]{1,0:T(8,128)(2,1)S(1)}, u32[]{:S(2)}) copy-start(bf16[896,512]{1,0:T(8,128)(2,1)S(1)} %get-tuple-element.11.pre_w) | copy-start | bytes 2752516
  19.5 0.6 %copy-start.4 = (bf16[384,128]{1,0:T(8,128)(2,1)}, bf16[384,128]{1,0:T(8,128)(2,1)S(1)}, u32[]{:S(2)}) copy-start(bf16[384,128]{1,0:T(8,128)(2,1)S(1)} %get-tuple-element.9.mel_ref) | copy-start | bytes 294916
  20.1 0.6 %copy-start.5 = (s32[16,8,128]{2,1,0:T(8,128)}, s32[16,8,128]{2,1,0:T(8,128)S(1)}, u32[]{:S(2)}) copy-start(s32[16,8,128]{2,1,0:T(8,128)S(1)} %get-tuple-element.10.dur_ref) | copy-start | bytes 196612

commit v2 on v1

--- a/solution.py
+++ b/solution.py
@@ -14,16 +14,20 @@
 MIB = 1024 * 1024
 
 
+def in_hbm(*arrays):
+    return [pltpu.with_memory_space_constraint(a, pltpu.HBM) for a in arrays]
+
+
 def leaky(v):
     return jnp.maximum(v, 0.1 * v)
 
 
 def gather_kernel(
     count,
-    dur_ref,
-    hidden_ref,
-    mel_w_ref,
-    mel_b_ref,
+    dur_hbm,
+    hidden_hbm,
+    mel_w_hbm,
+    mel_b_hbm,
     pre_w_hbm,
     up_w_hbm,
     mel_out,
@@ -38,6 +42,10 @@
     pre_w,
     up_w,
     spread,
+    dur_ref,
+    hidden_ref,
+    mel_w_ref,
+    mel_b_ref,
     load_sem,
     send_dur,
     recv_dur,
@@ -47,8 +55,21 @@
     me = lax.axis_index("tm")
     load_pre = pltpu.make_async_copy(pre_w_hbm, pre_w, load_sem.at[0])
     load_up = pltpu.make_async_copy(up_w_hbm, up_w, load_sem.at[1])
+    first_loads = [
+        pltpu.make_async_copy(source, target, load_sem.at[2 + i])
+        for i, (source, target) in enumerate(
+            (
+                (dur_hbm, dur_ref),
+                (hidden_hbm, hidden_ref),
+                (mel_w_hbm, mel_w_ref),
+                (mel_b_hbm, mel_b_ref),
+            )
+        )
+    ]
+    for load in first_loads:
+        load.start()
+    load_pre.start()
     load_up.start()
-    load_pre.start()
     barrier = pltpu.get_barrier_semaphore()
     for d in range(1, count):
         pl.semaphore_signal(
@@ -58,10 +79,17 @@
             device_id_type=pl.DeviceIdType.MESH,
         )
     phonemes = hidden_ref.shape[0]
-    channels = mel_w_ref.shape[1]
+    channels = mel_w_ref.shape[0]
+    for load in first_loads:
+        load.wait()
     dur_own[...] = jnp.zeros_like(dur_own)
     dur_own[0:1, 0:phonemes] = dur_ref[...]
-    mel = jnp.dot(hidden_ref[...], mel_w_ref[...], preferred_element_type=jnp.float32)
+    mel = lax.dot_general(
+        hidden_ref[...],
+        mel_w_ref[...],
+        (((1,), (1,)), ((), ())),
+        preferred_element_type=jnp.float32,
+    )
     mel = (mel + mel_b_ref[...]).astype(jnp.bfloat16)
     mel_own[...] = jnp.zeros_like(mel_own)
     mel_own[:, 0:channels] = mel
@@ -133,14 +161,16 @@
     mel_ref,
     dur_ref,
     pre_w,
+    up_w,
+    pre_b_hbm,
+    up_b_hbm,
+    res_hbm,
+    res_b_hbm,
+    out_hbm,
     pre_b,
-    up_hbm,
     up_b,
-    res_hbm,
+    res_w,
     res_b,
-    out_hbm,
-    up_w,
-    res_w,
     mel32,
     act32,
     x,
@@ -157,10 +187,14 @@
     f32 = jnp.float32
     rows = frames + 2 * HALO
     me = lax.axis_index("tm")
-    load_up = pltpu.make_async_copy(up_hbm, up_w, load_sem.at[0])
-    load_res = pltpu.make_async_copy(res_hbm, res_w, load_sem.at[1])
-    load_up.start()
-    load_res.start()
+    loads = [
+        pltpu.make_async_copy(source, target, load_sem.at[i])
+        for i, (source, target) in enumerate(
+            ((pre_b_hbm, pre_b), (up_b_hbm, up_b), (res_b_hbm, res_b), (res_hbm, res_w))
+        )
+    ]
+    for load in loads:
+        load.start()
     inside_low = me > 0
     inside_high = me < count - 1
 
@@ -209,6 +243,8 @@
         )
         mel32[PAD + r : PAD + r + n, :] = jnp.dot(hot, mel_ref[...], preferred_element_type=f32)
 
+    for load in loads[:3]:
+        load.wait()
     for r, n in chunks:
         taps = jnp.concatenate(
             [mel32[PAD + r + k - 3 : PAD + r + k - 3 + n, :].astype(bf) for k in range(7)], axis=1
@@ -224,7 +260,6 @@
         if p >= 8 - dil:
             xt_sh[p - 2, PAD + r : PAD + r + n, :] = edges(v, r)
 
-    load_up.wait()
     for r, n in chunks:
         here = act32[PAD + r : PAD + r + n, :].astype(bf)
         prior = act32[PAD + r - 1 : PAD + r - 1 + n, :].astype(bf)
@@ -268,7 +303,7 @@
                 if p in (0, 7):
                     c_sh[c_index(p), PAD + r : PAD + r + n, :] = edges(v, r)
 
-    load_res.wait()
+    loads[3].wait()
     inner(0, 1)
     for r, n in chunks:
         for p in range(8):
@@ -318,7 +353,7 @@
     width = up_weight.shape[2]
     bf, f32, i32 = jnp.bfloat16, jnp.float32, jnp.int32
     vmem = pl.BlockSpec(memory_space=pltpu.VMEM)
-    hbm = pl.BlockSpec(memory_space=pl.ANY)
+    hbm = pl.BlockSpec(memory_space=pltpu.HBM)
     dma = pltpu.SemaphoreType.DMA
     mel_near, dur_all, pre_w, up_w = pl.pallas_call(
         functools.partial(gather_kernel, count),
@@ -328,7 +363,7 @@
             jax.ShapeDtypeStruct((taps * LANES, inner), bf),
             jax.ShapeDtypeStruct((TAPS, inner, width), bf),
         ),
-        in_specs=[vmem, vmem, vmem, vmem, hbm, hbm],
+        in_specs=[hbm] * 6,
         out_specs=(vmem, vmem, vmem, vmem),
         scratch_shapes=[
             pltpu.VMEM((phonemes, LANES), bf),
@@ -339,7 +374,11 @@
             pltpu.VMEM(pre_weight.shape, bf),
             pltpu.VMEM(up_weight.shape, bf),
             pltpu.VMEM((2, 32 * TAPS, LANES), f32),
-            dma((2,)),
+            pltpu.VMEM((1, phonemes), i32),
+            pltpu.VMEM(hidden.shape, bf),
+            pltpu.VMEM(mel_weight.shape[::-1], bf),
+            pltpu.VMEM((1, channels), f32),
+            dma((6,)),
             dma((count,)),
             dma((count,)),
             dma((2,)),
@@ -349,18 +388,29 @@
             collective_id=0, has_side_effects=True, vmem_limit_bytes=24 * MIB
         ),
         name="gather_states",
-    )(durations.reshape(1, -1), hidden, mel_weight, mel_bias.reshape(1, -1), pre_weight, up_weight)
+    )(
+        *in_hbm(
+            durations.reshape(1, -1),
+            hidden,
+            mel_weight.T,
+            mel_bias.reshape(1, -1),
+            pre_weight,
+            up_weight,
+        )
+    )
 
     rows = frames + 2 * HALO
     chunk = rows // 3
     return pl.pallas_call(
         functools.partial(main_kernel, count, frames, chunk),
         out_shape=jax.ShapeDtypeStruct((frames * 8, width), bf),
-        in_specs=[vmem, vmem, vmem, vmem, hbm, vmem, hbm, vmem],
+        in_specs=[vmem] * 4 + [hbm] * 4,
         out_specs=hbm,
         scratch_shapes=[
-            pltpu.VMEM(up_w.shape, bf),
+            pltpu.VMEM((1, inner), f32),
+            pltpu.VMEM((1, width), f32),
             pltpu.VMEM(res_weight.shape, bf),
+            pltpu.VMEM(res_bias.shape, f32),
             pltpu.VMEM((rows + 2 * PAD, LANES), f32),
             pltpu.VMEM((rows + 2 * PAD, inner), f32),
             pltpu.VMEM((8, rows, width), bf),
@@ -370,20 +420,17 @@
             pltpu.VMEM((2, rows + 2 * PAD, width), f32),
             pltpu.VMEM((2, 2, frames * 2, LANES), f32),
             pltpu.VMEM((frames * 8, width), bf),
-            dma((2,)),
+            dma((4,)),
             dma((4,)),
         ],
-        compiler_params=pltpu.CompilerParams(vmem_limit_bytes=56 * MIB),
+        compiler_params=pltpu.CompilerParams(vmem_limit_bytes=44 * MIB),
         name="vocoder_section",
     )(
         mel_near,
         dur_all,
         pre_w,
-        pre_bias.reshape(1, -1),
         up_w,
-        up_bias.reshape(1, -1),
-        res_weight,
-        res_bias,
+        *in_hbm(pre_bias.reshape(1, -1), up_bias.reshape(1, -1), res_weight, res_bias),
     )
 
 

time: 45.7 us -> 33.7 us (0.74)
  local copies, waits for them, and re-layouts: 10.4 us -> 0 us
  Pallas kernels: 34.8 us -> 33.3 us
    unnamed x19 -> x0, local copies, waits for them, and re-layouts: 10.4 us -> none
    pallas_call x1, Pallas kernels: 24.5 us -> 23.4 us  [on_device(): pl.pallas_call(functools.partial(main_kernel, count, frames, chunk), out_...]
where the time goes in v2:
time: 33.7 us; the launch traced here: 33.5 us
  Pallas kernels  33.3 us (99%)
    pallas_call x1, Pallas kernels, on_device(): pl.pallas_call(functools.partial(main_kernel, count, frames, chunk), out_...  23.4 us
    pallas_call x1, Pallas kernels, on_device(): pl.pallas_call(functools.partial(gather_kernel, count), out_shape=(jax.Sh...  9.92 us

profile of v2, /device:TPU:0, one launch (start us, length us, event | category | flops | bytes accessed | tf_op | source)
XLA Modules:
  0.0 33.5 jit_solution(3640730971743211662)
XLA Ops:
  0.0 9.9 %gather_states.1 = (bf16[384,128]{1,0:T(8,128)(2,1)S(1)}, s32[16,8,128]{2,1,0:T(8,128)S(1)}, bf16[896,512]{1,0:T(8,128)(2,1)S(1)}, bf16[16,512,256]{2,1,0:T(8,128)(2,1)S(1)}) custom-call(s32[1,32]{1,0:T(1,128)} %bitcast.8, bf16[32,512]{1,0:T(8,128)(2,1)} %hidden_hbm.1, bf16[80,512]{1,0:T(8,128)(2,1)} %bitcast.5, f32[1,80]{1,0:T(1,128)} %bitcast.9, ...), custom_call_target="tpu_custom_call" | custom-call | tf_op jit(solution)/shard_map/gather_states/pallas_call | solution.py:358
  9.9 23.4 %vocoder_section.1 = bf16[8192,256]{1,0:T(8,128)(2,1)} custom-call(bf16[384,128]{1,0:T(8,128)(2,1)S(1)} %get-tuple-element.9.mel_ref, s32[16,8,128]{2,1,0:T(8,128)S(1)} %get-tuple-element.10.dur_ref, bf16[896,512]{1,0:T(8,128)(2,1)S(1)} %get-tuple-element.11.pre_w, bf16[16,512,256]{2,1,0:T(8,128)(2,1)S(1)} %get-tuple-element.12.up_w, f32[1,512]{1,0:T(1,128)} %bitcast.6, ...), custom_call_target="tpu_custom_call" | custom-call | tf_op jit(solution)/shard_map/vocoder_section/pallas_call | solution.py:404

commit v3 on v2

--- a/solution.py
+++ b/solution.py
@@ -313,9 +313,9 @@
             x[p, r : r + n, :] = value
             put_xt(value, p, r, n, 3)
     inner(2, 3)
-    n = frames // 4
+    n = frames // 8
     stores = []
-    for i in range(4):
+    for i in range(8):
         r = HALO + i * n
         for p in range(8):
             lhs = gathered(c, c_sh, c_index, p, 1, r, n)
@@ -400,7 +400,7 @@
     )
 
     rows = frames + 2 * HALO
-    chunk = rows // 3
+    chunk = rows // 6
     return pl.pallas_call(
         functools.partial(main_kernel, count, frames, chunk),
         out_shape=jax.ShapeDtypeStruct((frames * 8, width), bf),
@@ -418,10 +418,10 @@
             pltpu.VMEM((8, rows, width), bf),
             pltpu.VMEM((6, rows + 2 * PAD, width), f32),
             pltpu.VMEM((2, rows + 2 * PAD, width), f32),
-            pltpu.VMEM((2, 2, frames * 2, LANES), f32),
+            pltpu.VMEM((2, 2, frames * 8 // 8, LANES), f32),
             pltpu.VMEM((frames * 8, width), bf),
             dma((4,)),
-            dma((4,)),
+            dma((8,)),
         ],
         compiler_params=pltpu.CompilerParams(vmem_limit_bytes=44 * MIB),
         name="vocoder_section",

time: 33.7 us -> 33.4 us (level)
    pallas_call x1, Pallas kernels: 23.4 us -> 23.1 us  [on_device(): pl.pallas_call(functools.partial(main_kernel, count, frames, chunk), out_...]
where the time goes in v3:
time: 33.4 us; the launch traced here: 33.2 us
  Pallas kernels  33 us (99%)
    pallas_call x1, Pallas kernels, on_device(): pl.pallas_call(functools.partial(main_kernel, count, frames, chunk), out_...  23.1 us
    pallas_call x1, Pallas kernels, on_device(): pl.pallas_call(functools.partial(gather_kernel, count), out_shape=(jax.Sh...  9.92 us

profile of v3, /device:TPU:0, one launch (start us, length us, event | category | flops | bytes accessed | tf_op | source)
XLA Modules:
  0.0 33.2 jit_solution(4484047235748322634)
XLA Ops:
  0.0 9.9 %gather_states.1 = (bf16[384,128]{1,0:T(8,128)(2,1)S(1)}, s32[16,8,128]{2,1,0:T(8,128)S(1)}, bf16[896,512]{1,0:T(8,128)(2,1)S(1)}, bf16[16,512,256]{2,1,0:T(8,128)(2,1)S(1)}) custom-call(s32[1,32]{1,0:T(1,128)} %bitcast.8, bf16[32,512]{1,0:T(8,128)(2,1)} %hidden_hbm.1, bf16[80,512]{1,0:T(8,128)(2,1)} %bitcast.5, f32[1,80]{1,0:T(1,128)} %bitcast.9, ...), custom_call_target="tpu_custom_call" | custom-call | tf_op jit(solution)/shard_map/gather_states/pallas_call | solution.py:358
  9.9 23.1 %vocoder_section.1 = bf16[8192,256]{1,0:T(8,128)(2,1)} custom-call(bf16[384,128]{1,0:T(8,128)(2,1)S(1)} %get-tuple-element.9.mel_ref, s32[16,8,128]{2,1,0:T(8,128)S(1)} %get-tuple-element.10.dur_ref, bf16[896,512]{1,0:T(8,128)(2,1)S(1)} %get-tuple-element.11.pre_w, bf16[16,512,256]{2,1,0:T(8,128)(2,1)S(1)} %get-tuple-element.12.up_w, f32[1,512]{1,0:T(1,128)} %bitcast.6, ...), custom_call_target="tpu_custom_call" | custom-call | tf_op jit(solution)/shard_map/vocoder_section/pallas_call | solution.py:404
